TPU v7x, 32 devices: a whole 2x2x4 slice. The times are simulated.
32 devices in a mesh: rows: 8 (over z, x), grp: 4 (over y, core).
Axes of the slice: x: 2, y: 2, z: 4, core: 2. Of those that a mesh axis runs over, the one named last changes fastest.
Arguments:
- embeddings: bfloat16 [131072, 1024], P(('rows', 'grp')), may hold values from -6 to 6
- residual: float32 [131072, 64], P(('rows', 'grp')), may hold values from -6 to 6
- block_ids: int32 [512], replicated, may hold values from 0 to 131071, as said below
Outputs:
- updated: float32 [131072, 64], P(('rows', 'grp'))
- change: float32 [512, 64], replicated
Inputs may be any that keep to these rules, and one draw needn't show every extreme that they name: `block_ids`: 512 distinct row ids in increasing order; at most 32 of them lie in one device's 4096 consecutive rows, and some device holds exactly 32.
All inputs are finite; a program needn't handle non-finite values.
Results may differ from a plain program's by a relative error of at most 0.0065.
Values may be sent and summed in bfloat16 or wider, within the bound.
A program may use at most 64 MiB of HBM per device.

v0:
```python
import functools
import jax
import jax.numpy as jnp
from jax import lax
from jax.experimental import pallas as pl
from jax.experimental.pallas import tpu as pltpu
from jax.sharding import PartitionSpec as P

ridge_weight = 0.5
TILE = 128
STEP = 8
HIGH = lax.Precision.HIGHEST


def small_inverse(entries, n):
    a = {k: v for k, v in entries.items()}
    get = lambda i, j: a[(min(i, j), max(i, j))]
    for k in range(n):
        d = 1.0 / get(k, k)
        col = {i: get(i, k) for i in range(n) if i != k}
        scaled = {i: col[i] * d for i in col}
        for i in range(n):
            for j in range(i, n):
                if i != k and j != k:
                    a[(i, j)] = a[(i, j)] - scaled[i] * col[j]
        for i in col:
            a[(min(i, k), max(i, k))] = scaled[i]
        a[(k, k)] = -d
    return {k: -v for k, v in a.items()}


def tile_inverse(m):
    lane = lax.broadcasted_iota(jnp.int32, (8, TILE), 1)
    sub = lax.broadcasted_iota(jnp.int32, (8, TILE), 0)
    m = list(m)
    groups = TILE // 8
    for p in range(groups):
        c0 = p * STEP
        panel = m[p]
        entries = {
            (i, j): jnp.broadcast_to(panel[i:i + 1, c0 + j:c0 + j + 1], (8, TILE))
            for i in range(STEP) for j in range(i, STEP)
        }
        inv = small_inverse(entries, STEP)
        inside = (lane >= c0) & (lane < c0 + STEP)
        unit = jnp.where(lane - c0 == sub, 1.0, 0.0)
        augmented = jnp.where(inside, unit, panel)
        rows = [jnp.broadcast_to(augmented[j:j + 1, :], (8, TILE)) for j in range(STEP)]
        new_rows = []
        for i in range(STEP):
            acc = None
            for j in range(STEP):
                term = inv[(min(i, j), max(i, j))] * rows[j]
                acc = term if acc is None else acc + term
            new_rows.append(acc)
        for v in range(groups):
            if v == p:
                continue
            acc = jnp.where(inside, 0.0, m[v])
            for j in range(STEP):
                coef = jnp.broadcast_to(m[v][:, c0 + j:c0 + j + 1], (8, TILE))
                acc = acc - coef * new_rows[j]
            m[v] = acc
        acc = new_rows[0]
        for j in range(1, STEP):
            acc = jnp.where(sub == j, new_rows[j], acc)
        m[p] = acc
    return m


def dot(a, b, dims=((1,), (0,))):
    return lax.dot_general(a, b, (dims, ((), ())), precision=HIGH, preferred_element_type=jnp.float32)


def gram_kernel(cross, width):
    n = cross.shape[0]
    eye = (lax.broadcasted_iota(jnp.int32, (n, n), 0) == lax.broadcasted_iota(jnp.int32, (n, n), 1))
    diag = jnp.where(eye, cross, 0.0)
    row_norms = jnp.sum(diag, axis=0, keepdims=True)
    col_norms = jnp.sum(diag, axis=1, keepdims=True)
    dist = jnp.maximum(col_norms + row_norms - 2.0 * cross, 0.0)
    return jnp.exp(dist * (-2.0 / width)) + jnp.where(eye, ridge_weight, 0.0), row_norms


def gather_index(ids_row, rows_here, slots):
    n = ids_row.shape[1]
    owners_row = owner_of(ids_row, rows_here).astype(jnp.float32)
    same = lax.broadcasted_iota(jnp.int32, (n, n), 0) == lax.broadcasted_iota(jnp.int32, (n, n), 1)
    owners = jnp.sum(jnp.where(same, owners_row, 0.0), axis=1, keepdims=True)
    before = jnp.sum(jnp.where(owners_row < owners, 1.0, 0.0), axis=1, keepdims=True)
    position = lax.broadcasted_iota(jnp.int32, (n, 1), 0)
    return owners.astype(jnp.int32) * slots + position - before.astype(jnp.int32)


def owner_of(ids, rows_here):
    if rows_here & (rows_here - 1) == 0:
        return lax.shift_right_logical(ids, jnp.full_like(ids, rows_here.bit_length() - 1))
    return lax.div(ids, jnp.full_like(ids, rows_here))


def solve_kernel(rows_here, capacity, ids_ref, gathered_ref, emb_ref, norms_ref, change_ref, a_ref, r_ref, inv_ref):
    n, width = emb_ref.shape
    outs = change_ref.shape[0]
    slots = gathered_ref.shape[0]
    index = gather_index(ids_ref[...], rows_here, capacity)
    pick = jnp.where(lax.broadcasted_iota(jnp.int32, (n, slots), 1) == index, 1.0, 0.0).astype(jnp.bfloat16)
    block = jnp.dot(pick, gathered_ref[...], preferred_element_type=jnp.float32)
    emb = block[:, :width].astype(jnp.bfloat16)
    emb_ref[...] = emb
    res = block[:, width:width + outs] + block[:, width + outs:width + 2 * outs]
    r_ref[...] = res
    cross = lax.dot_general(emb, emb, (((1,), (1,)), ((), ())), preferred_element_type=jnp.float32)
    a, row_norms = gram_kernel(cross, width)
    norms_ref[...] = jnp.broadcast_to(row_norms, norms_ref.shape)
    a_ref[...] = a
    tiles = n // TILE
    groups = TILE // 8

    def factor(k, carry):
        here = pl.ds(pl.multiple_of(k * TILE, TILE), TILE)
        m = [a_ref[pl.ds(pl.multiple_of(k * TILE + 8 * v, 8), 8), here] for v in range(groups)]
        m = tile_inverse(m)
        for v in range(groups):
            inv_ref[k, 8 * v:8 * v + 8, :] = m[v]
        inv = inv_ref[k]
        right = a_ref[here, :]
        scaled = dot(inv, right)
        scaled_res = dot(inv, r_ref[here, :])
        rows_after = lax.broadcasted_iota(jnp.int32, (n, 1), 0) >= (k + 1) * TILE
        left = jnp.where(rows_after, a_ref[:, here], 0.0)
        a_ref[...] = a_ref[...] - dot(left, scaled)
        r_ref[...] = r_ref[...] - dot(left, scaled_res)
        return carry

    lax.fori_loop(0, tiles, factor, 0)
    for k in range(tiles - 1, -1, -1):
        lo, hi = k * TILE, (k + 1) * TILE
        rest = r_ref[lo:hi, :]
        if hi < n:
            rest = rest - dot(a_ref[lo:hi, hi:], r_ref[hi:, :])
        r_ref[lo:hi, :] = dot(inv_ref[k], rest)
    change_ref[...] = r_ref[...].T


def solve(ids, gathered, rows_here, capacity, width, outs):
    n = ids.shape[0]
    vm = pl.BlockSpec(memory_space=pltpu.VMEM)
    return pl.pallas_call(
        functools.partial(solve_kernel, rows_here, capacity),
        out_shape=(
            jax.ShapeDtypeStruct((n, width), jnp.bfloat16),
            jax.ShapeDtypeStruct((8, n), jnp.float32),
            jax.ShapeDtypeStruct((outs, n), jnp.float32),
        ),
        in_specs=[vm, vm],
        out_specs=(vm, vm, vm),
        scratch_shapes=[
            pltpu.VMEM((n, n), jnp.float32),
            pltpu.VMEM((n, outs), jnp.float32),
            pltpu.VMEM((n // TILE, TILE, TILE), jnp.float32),
        ],
        compiler_params=pltpu.CompilerParams(vmem_limit_bytes=48 * 2**20),
        name="solve",
    )(ids.reshape(1, n), gathered)


def update_kernel(base_ref, ids_ref, emb_ref, block_ref, norms_ref, change_ref, res_ref, out_ref):
    step = pl.program_id(0)
    rows, width = emb_ref.shape
    emb = emb_ref[...]
    wide = emb.astype(jnp.float32)
    row_norms = jnp.sum(wide * wide, axis=1, keepdims=True)
    cross = lax.dot_general(emb, block_ref[...], (((1,), (1,)), ((), ())), preferred_element_type=jnp.float32)
    dist = jnp.maximum(row_norms + norms_ref[0:1, :] - 2.0 * cross, 0.0)
    columns = jnp.exp(dist * (-2.0 / width))
    row = base_ref[0] + step * rows + lax.broadcasted_iota(jnp.int32, (rows, 1), 0)
    columns = columns + jnp.where(row == ids_ref[...], ridge_weight, 0.0)
    out_ref[...] = res_ref[...] - lax.dot_general(
        change_ref[...].astype(jnp.bfloat16), columns.astype(jnp.bfloat16),
        (((1,), (1,)), ((), ())), preferred_element_type=jnp.float32)


def update(base, ids, emb, block, norms, change, res_t, rows_step=512):
    rows, width = emb.shape
    n = block.shape[0]
    outs = res_t.shape[0]
    whole = lambda shape: pl.BlockSpec(shape, lambda i: (0, 0))
    return pl.pallas_call(
        update_kernel,
        grid=(rows // rows_step,),
        out_shape=jax.ShapeDtypeStruct((outs, rows), jnp.float32),
        in_specs=[
            pl.BlockSpec(memory_space=pltpu.SMEM),
            whole((1, n)),
            pl.BlockSpec((rows_step, width), lambda i: (i, 0)),
            whole((n, width)), whole((8, n)), whole((outs, n)),
            pl.BlockSpec((outs, rows_step), lambda i: (0, i)),
        ],
        out_specs=pl.BlockSpec((outs, rows_step), lambda i: (0, i)),
        compiler_params=pltpu.CompilerParams(vmem_limit_bytes=48 * 2**20),
        name="update",
    )(base, ids.reshape(1, n), emb, block, norms, change, res_t)


def pack_kernel(base_ref, ids_ref, emb_ref, res_ref, out_ref, buf_ref, sems):
    n = ids_ref.shape[0]
    outs, rows = res_ref.shape
    slots, total = out_ref.shape
    width = total - 2 * outs
    base = base_ref[0]
    first = jnp.int32(0)
    jump = 1 << (n.bit_length() - 1)
    while jump:
        ahead = first + jump
        value = ids_ref[jnp.minimum(ahead, n) - 1]
        first = jnp.where((ahead <= n) & (value < base), ahead, first)
        jump //= 2
    slot = lax.broadcasted_iota(jnp.int32, (slots, 1), 0)
    local = jnp.zeros((slots, 1), jnp.int32)
    copies = []
    for s in range(slots):
        row = jnp.clip(ids_ref[jnp.minimum(first + s, n - 1)] - base, 0, rows - 1)
        local = jnp.where(slot == s, row, local)
        group = pl.multiple_of((row >> 4) << 4, 16)
        copy = pltpu.make_async_copy(emb_ref.at[pl.ds(group, 16)], buf_ref.at[pl.ds(16 * s, 16)], sems.at[s])
        copy.start()
        copies.append(copy)
    res = res_ref[...]
    high = res.astype(jnp.bfloat16)
    low = (res - high.astype(jnp.float32)).astype(jnp.bfloat16)
    pick = jnp.where(lax.broadcasted_iota(jnp.int32, (slots, rows), 1) == local, 1.0, 0.0).astype(jnp.bfloat16)
    nt = (((1,), (1,)), ((), ()))
    high_rows = lax.dot_general(pick, high, nt, preferred_element_type=jnp.float32)
    low_rows = lax.dot_general(pick, low, nt, preferred_element_type=jnp.float32)
    out_ref[:, width:] = jnp.concatenate([high_rows, low_rows], axis=1).astype(jnp.bfloat16)
    for copy in copies:
        copy.wait()
    wanted = 16 * slot + (local & 15)
    pick = jnp.where(lax.broadcasted_iota(jnp.int32, (slots, 16 * slots), 1) == wanted, 1.0, 0.0).astype(jnp.bfloat16)
    out_ref[:, :width] = jnp.dot(pick, buf_ref[...], preferred_element_type=jnp.float32).astype(jnp.bfloat16)


def pack(base, ids, emb, res_t, slots):
    width = emb.shape[1]
    outs = res_t.shape[0]
    return pl.pallas_call(
        pack_kernel,
        out_shape=jax.ShapeDtypeStruct((slots, width + 2 * outs), jnp.bfloat16),
        in_specs=[
            pl.BlockSpec(memory_space=pltpu.SMEM), pl.BlockSpec(memory_space=pltpu.SMEM),
            pl.BlockSpec(memory_space=pl.ANY), pl.BlockSpec(memory_space=pltpu.VMEM),
        ],
        out_specs=pl.BlockSpec(memory_space=pltpu.VMEM),
        scratch_shapes=[pltpu.VMEM((16 * slots, width), jnp.bfloat16), pltpu.SemaphoreType.DMA((slots,))],
        compiler_params=pltpu.CompilerParams(vmem_limit_bytes=32 * 2**20),
        name="pack",
    )(base, ids, emb, res_t)


def gather(packed):
    return lax.all_gather(packed, ("rows", "grp"), axis=0, tiled=True)


def on_device(embeddings, residual, block_ids):
    rows_here, width = embeddings.shape
    outs = residual.shape[1]
    n = block_ids.shape[0]
    group_size = lax.axis_size("grp")
    devices = lax.axis_size("rows") * group_size
    slots = max(16, 2 * n // devices)
    base = ((lax.axis_index("rows") * group_size + lax.axis_index("grp")) * rows_here).astype(jnp.int32).reshape(1)
    res_t = residual.T
    packed = pack(base, block_ids, embeddings, res_t, slots)
    gathered = gather(packed)
    block_emb, norms, change_t = solve(block_ids, gathered, rows_here, slots, width, outs)
    updated_t = update(base, block_ids, embeddings, block_emb, norms, change_t, res_t)
    return (updated_t.T, change_t.T)


def solution(mesh):
    placed = (P(("rows", "grp"), None), P(("rows", "grp"), None), P())
    return jax.shard_map(
        on_device,
        mesh=mesh,
        in_specs=placed,
        out_specs=(P(("rows", "grp"), None), P()),
        check_vma=False,
    )
```

profile of v0, /device:TPU:0, one launch (start us, length us, event | category | flops | bytes accessed | tf_op | source)
XLA Modules:
  0.0 132.1 jit_solution(17894554722616726508)
XLA Ops:
  7.2 0.0 copy-start.6
  7.2 0.0 all-gather.2.cloned.1.call-start
  7.2 0.0 copy-start
  7.2 3.4 %copy-done = bf16[4096,1024]{1,0:T(8,128)(2,1)S(1)} copy-done((bf16[4096,1024]{1,0:T(8,128)(2,1)S(1)}, bf16[4096,1024]{1,0:T(8,128)(2,1)}, u32[]{:S(2)}) %copy-start) | copy-done | bytes 8388632
  10.6 0.0 copy-start.1
  10.6 1.2 copy-done.1
  11.8 0.0 copy-start.5
  11.8 0.7 copy-done.5
  12.5 0.0 copy-start.2
  12.5 4.0 %pack.1 = bf16[32,1152]{1,0:T(8,128)(2,1)} custom-call(s32[1]{0:T(128)} %bitcast.base_ref, s32[512]{0:T(512)S(1)} %copy-done.5, bf16[4096,1024]{1,0:T(8,128)(2,1)S(1)} %copy-done, f32[64,4096]{1,0:T(8,128)S(1)} %bitcast.5), custom_call_target="tpu_custom_call" | custom-call | tf_op jit(solution)/shard_map/pack/pallas_call | solution.py:246
  16.6 0.0 all-gather.2.cloned.1.call-update
  16.6 60.1 %all-gather.2.cloned.1.call-done.gathered_ref = bf16[1024,1152]{1,0:T(8,128)(2,1)} async-done(((bf16[32,1152]{1,0:T(8,128)(2,1)}), bf16[1024,1152]{1,0:T(8,128)(2,1)}) %all-gather.2.cloned.1.call-update) | async-done | bytes 2359312 | tf_op jit(solution)/shard_map/all_gather | solution.py:261
  76.7 0.0 copy-done.6
  76.7 0.0 copy-start.3
  76.7 1.7 %copy-done.3 = bf16[1024,1152]{1,0:T(8,128)(2,1)S(1)} copy-done((bf16[1024,1152]{1,0:T(8,128)(2,1)S(1)}, bf16[1024,1152]{1,0:T(8,128)(2,1)}, u32[]{:S(2)}) %copy-start.3) | copy-done | bytes 2359320
  78.4 34.1 %solve.1 = (bf16[512,1024]{1,0:T(8,128)(2,1)S(1)}, f32[8,512]{1,0:T(8,128)S(1)}, f32[64,512]{1,0:T(8,128)}) custom-call(s32[1,512]{1,0:T(1,128)S(1)} %bitcast.8, bf16[1024,1152]{1,0:T(8,128)(2,1)S(1)} %copy-done.3), custom_call_target="tpu_custom_call" | custom-call | tf_op jit(solution)/shard_map/solve/pallas_call | solution.py:148
  112.5 0.0 copy-done.2
  112.5 0.0 copy-start.4
  112.6 0.9 copy-done.4
  113.5 11.8 %update.1 = f32[64,4096]{1,0:T(8,128)} custom-call(s32[1]{0:T(128)} %bitcast.base_ref, s32[1,512]{1,0:T(1,128)S(1)} %bitcast.9, bf16[4096,1024]{1,0:T(8,128)(2,1)} %emb_ref.3, bf16[512,1024]{1,0:T(8,128)(2,1)S(1)} %get-tuple-element.5.block_ref, f32[8,512]{1,0:T(8,128)S(1)} %get-tuple-element.6.norms_ref, f32[64,512]{1,0:T(8,128)S(1)} %copy-done.4, ...), custom_call_target="tpu_custom_call" | custom-call | tf_op jit(solution)/shard_map/update/pallas_call | solution.py:188
Async XLA Ops:
  7.2 69.6 %copy-start.6 = (s32[512]{0:T(512)S(1)}, s32[512]{0:T(512)}, u32[]{:S(2)}) copy-start(s32[512]{0:T(512)} %ids_ref.1) | copy-start | bytes 6148
  7.2 69.6 %all-gather.2.cloned.1.call-start = ((), (), s32[]{:S(2)}) async-start(), calls=%async_computation | async-start | bytes 2433024 | tf_op jit(solution)/shard_map/all_gather | solution.py:261
  7.2 3.4 %copy-start = (bf16[4096,1024]{1,0:T(8,128)(2,1)S(1)}, bf16[4096,1024]{1,0:T(8,128)(2,1)}, u32[]{:S(2)}) copy-start(bf16[4096,1024]{1,0:T(8,128)(2,1)} %emb_ref.3) | copy-start | bytes 25165828
  10.6 1.2 copy-start.1
  11.8 0.7 copy-start.5
  12.5 100.0 %copy-start.2 = (f32[4096,64]{0,1:T(8,128)S(1)}, f32[4096,64]{0,1:T(8,128)}, u32[]{:S(2)}) copy-start(f32[4096,64]{0,1:T(8,128)} %param.4) | copy-start | bytes 3145732
  76.7 1.7 %copy-start.3 = (bf16[1024,1152]{1,0:T(8,128)(2,1)S(1)}, bf16[1024,1152]{1,0:T(8,128)(2,1)}, u32[]{:S(2)}) copy-start(bf16[1024,1152]{1,0:T(8,128)(2,1)} %all-gather.2.cloned.1.call-done.gathered_ref) | copy-start | bytes 7077892
  112.5 0.9 copy-start.4
Sparse Core Ops, SparseCore 0:
  16.7 59.9 all-gather.1
where the time goes:
time: 133 us; the launch traced here: 132 us
  waiting for transfers between devices  60.2 us (45%)
  Pallas kernels  49.9 us (38%)
  between operations  14.1 us (11%)
  local copies, waits for them, and re-layouts  7.86 us (6%)
    all_gather x1, waiting for transfers between devices, gather(): return lax.all_gather(packed, ('rows', 'grp'), axis=0, tiled=True)  60.1 us
    pallas_call x1, Pallas kernels, solve(): pl.pallas_call(functools.partial(solve_kernel, rows_here, capacity), out_...  34.1 us
    pallas_call x1, Pallas kernels, update(): pl.pallas_call(update_kernel, grid=(rows // rows_step,), out_shape=jax.Sh...  11.8 us
    unnamed x14, local copies, waits for them, and re-layouts  7.86 us
    pallas_call x1, Pallas kernels, pack(): pl.pallas_call(pack_kernel, out_shape=jax.ShapeDtypeStruct((slots, width...  4.04 us
  transfers between devices with their start and end apart: 1, of which 1 were waited for; matrix products, arithmetic and copies ran while one was open for 0% of the time, Pallas kernels for 0%

commit v1 on v0

--- a/solution.py
+++ b/solution.py
@@ -257,8 +257,103 @@
     )(base, ids, emb, res_t)
 
 
+def gather_kernel(shape, packed_ref, out_ref, send_sems, recv_sems):
+    n_far, n_side = shape
+    slots, total = packed_ref.shape
+    half = (total // 256) * 128
+    r, g = lax.axis_index("rows"), lax.axis_index("grp")
+    group = 2 * n_side
+    z, x, y, c = r // 2, r % 2, g // 2, g % 2
+    across = 1 - x
+    other = 1 - c
+
+    def place(z, x, y, c):
+        return pl.ds(pl.multiple_of(((2 * z + x) * group + 2 * y + c) * slots, slots), slots)
+
+    def device(z, x, y, c):
+        return (2 * z + x, 2 * y + c)
+
+    targets = [device((z + k) % n_far, x, y, c) for k in range(1, n_far)]
+    targets += [device(z, across, y, c), device(z, x, y, other)]
+    targets += [device(z, x, (y + j) % n_side, c) for j in range(1, n_side)]
+    barrier = pltpu.get_barrier_semaphore()
+    for target in targets:
+        pl.semaphore_signal(barrier, inc=1, device_id=target, device_id_type=pl.DeviceIdType.MESH)
+    pl.semaphore_wait(barrier, len(targets))
+    started = []
+
+    def send(source, region, target):
+        at = len(started)
+        copy = pltpu.make_async_remote_copy(
+            src_ref=source, dst_ref=out_ref.at[region], send_sem=send_sems.at[at], recv_sem=recv_sems.at[at],
+            device_id=target, device_id_type=pl.DeviceIdType.MESH)
+        copy.start()
+        started.append(copy)
+        return copy
+
+    own = place(z, x, y, c)
+    full, left, right = slice(0, total), slice(0, half), slice(half, total)
+    far, wide, deep, core = [], {}, {}, []
+    for k in range(1, n_far):
+        far.append(send(packed_ref, (own, full), device((z + k) % n_far, x, y, c)))
+
+    def spread(k, source, where):
+        wide[k] = send(source, (where, full), device(z, across, y, c))
+        for j in range(1, n_side):
+            deep[k, j] = send(source, (where, full), device(z, x, (y + j) % n_side, c))
+        core.append(send(source, (where, full), device(z, x, y, other)))
+
+    spread(0, packed_ref, own)
+    out_ref[own, :] = packed_ref[...]
+    corners = []
+
+    def turn(k):
+        from_z = (z - k + n_far) % n_far
+        wide[k].wait_recv()
+        here = place(from_z, across, y, c)
+        for j in range(1, n_side):
+            corners.append((send(out_ref.at[here, left], (here, left), device(z, x, (y + j) % n_side, c)),
+                            (place(from_z, across, (y - j + n_side) % n_side, c), left)))
+        core.append(send(out_ref.at[here, full], (here, full), device(z, x, y, other)))
+        for j in range(1, n_side):
+            deep[k, j].wait_recv()
+            here = place(from_z, x, (y - j + n_side) % n_side, c)
+            corners.append((send(out_ref.at[here, right], (here, right), device(z, across, y, c)),
+                            (place(from_z, across, (y - j + n_side) % n_side, c), right)))
+            core.append(send(out_ref.at[here, full], (here, full), device(z, x, y, other)))
+
+    for k in range(1, n_far):
+        far[k - 1].wait_recv()
+        here = place((z - k + n_far) % n_far, x, y, c)
+        spread(k, out_ref.at[here, full], here)
+        turn(k - 1)
+    turn(n_far - 1)
+    for copy, region in corners:
+        copy.wait_recv()
+        core.append(send(out_ref.at[region], region, device(z, x, y, other)))
+    for copy in core:
+        copy.wait_recv()
+    for copy in started:
+        copy.wait_send()
+
+
 def gather(packed):
-    return lax.all_gather(packed, ("rows", "grp"), axis=0, tiled=True)
+    n_rows, n_grp = lax.axis_size("rows"), lax.axis_size("grp")
+    n_far, n_side = n_rows // 2, n_grp // 2
+    slots, total = packed.shape
+    count = (n_far - 1) + n_far * (n_side + 1) + n_far * (3 * (n_side - 1) + 1)
+    count += 2 * n_far * (n_side - 1) + n_far
+    vm = pl.BlockSpec(memory_space=pltpu.VMEM)
+    return pl.pallas_call(
+        functools.partial(gather_kernel, (n_far, n_side)),
+        out_shape=jax.ShapeDtypeStruct((n_rows * n_grp * slots, total), packed.dtype),
+        in_specs=[vm],
+        out_specs=vm,
+        scratch_shapes=[pltpu.SemaphoreType.DMA((count,)), pltpu.SemaphoreType.DMA((count,))],
+        compiler_params=pltpu.CompilerParams(
+            collective_id=0, has_side_effects=True, vmem_limit_bytes=32 * 2**20),
+        name="gather",
+    )(packed)
 
 
 def on_device(embeddings, residual, block_ids):

time: 133 us -> 79.8 us (0.60)
  waiting for transfers between devices: 60.2 us -> 0 us
  Pallas kernels: 49.9 us -> 72.5 us
  between operations: 14.1 us -> 0.68 us
  local copies, waits for them, and re-layouts: 7.86 us -> 6.19 us
    all_gather x1 -> x0, waiting for transfers between devices: 60.1 us -> none  [gather(): return lax.all_gather(packed, ('rows', 'grp'), axis=0, tiled=True)]
    pallas_call x0 -> x1, Pallas kernels: none -> 23.1 us  [gather(): pl.pallas_call(functools.partial(gather_kernel, (n_far, n_side)), out_sha...]
    unnamed x14 -> x12, local copies, waits for them, and re-layouts: 7.86 us -> 6.19 us
  transfers between devices with their start and end apart: 1 -> 0, of which waited for: 1 -> 0; matrix products, arithmetic and copies ran while one was open for 0% -> 0% of each run, Pallas kernels for 0% -> 0%
where the time goes in v1:
time: 79.8 us; the launch traced here: 79.3 us
  Pallas kernels  72.5 us (91%)
  local copies, waits for them, and re-layouts  6.19 us (8%)
    pallas_call x1, Pallas kernels, solve(): pl.pallas_call(functools.partial(solve_kernel, rows_here, capacity), out_...  34.2 us
    pallas_call x1, Pallas kernels, gather(): pl.pallas_call(functools.partial(gather_kernel, (n_far, n_side)), out_sha...  23.1 us
    pallas_call x1, Pallas kernels, update(): pl.pallas_call(update_kernel, grid=(rows // rows_step,), out_shape=jax.Sh...  11.8 us
    unnamed x12, local copies, waits for them, and re-layouts  6.19 us
    pallas_call x1, Pallas kernels, pack(): pl.pallas_call(pack_kernel, out_shape=jax.ShapeDtypeStruct((slots, width...  3.41 us

profile of v1, /device:TPU:0, one launch (start us, length us, event | category | flops | bytes accessed | tf_op | source)
XLA Modules:
  0.0 79.3 jit_solution(5377019248568889321)
XLA Ops:
  0.6 0.0 copy-start.5
  0.6 0.0 copy-start
  0.7 3.4 %copy-done = bf16[4096,1024]{1,0:T(8,128)(2,1)S(1)} copy-done((bf16[4096,1024]{1,0:T(8,128)(2,1)S(1)}, bf16[4096,1024]{1,0:T(8,128)(2,1)}, u32[]{:S(2)}) %copy-start) | copy-done | bytes 8388632
  4.0 0.0 copy-start.1
  4.0 1.2 %copy-done.1 = f32[4096,64]{0,1:T(8,128)S(1)} copy-done((f32[4096,64]{0,1:T(8,128)S(1)}, f32[4096,64]{0,1:T(8,128)}, u32[]{:S(2)}) %copy-start.1) | copy-done | bytes 1048600
  5.3 0.0 copy-start.4
  5.3 0.7 copy-done.4
  5.9 0.0 copy-start.2
  5.9 3.4 %pack.1.packed_ref = bf16[32,1152]{1,0:T(8,128)(2,1)S(1)} custom-call(s32[1]{0:T(128)} %bitcast.base_ref, s32[512]{0:T(512)S(1)} %copy-done.4, bf16[4096,1024]{1,0:T(8,128)(2,1)S(1)} %copy-done, f32[64,4096]{1,0:T(8,128)S(1)} %bitcast.5), custom_call_target="tpu_custom_call" | custom-call | tf_op jit(solution)/shard_map/pack/pallas_call | solution.py:246
  9.4 23.1 %gather.1.gathered_ref = bf16[1024,1152]{1,0:T(8,128)(2,1)S(1)} custom-call(bf16[32,1152]{1,0:T(8,128)(2,1)S(1)} %pack.1.packed_ref), custom_call_target="tpu_custom_call" | custom-call | tf_op jit(solution)/shard_map/gather/pallas_call | solution.py:347
  32.5 0.0 copy-done.5
  32.5 34.2 %solve.1 = (bf16[512,1024]{1,0:T(8,128)(2,1)S(1)}, f32[8,512]{1,0:T(8,128)S(1)}, f32[64,512]{1,0:T(8,128)}) custom-call(s32[1,512]{1,0:T(1,128)S(1)} %bitcast.8, bf16[1024,1152]{1,0:T(8,128)(2,1)S(1)} %gather.1.gathered_ref), custom_call_target="tpu_custom_call" | custom-call | tf_op jit(solution)/shard_map/solve/pallas_call | solution.py:148
  66.7 0.0 copy-done.2
  66.7 0.0 copy-start.3
  66.7 0.9 %copy-done.3 = f32[64,512]{1,0:T(8,128)S(1)} copy-done((f32[64,512]{1,0:T(8,128)S(1)}, f32[64,512]{1,0:T(8,128)}, u32[]{:S(2)}) %copy-start.3) | copy-done | bytes 131096
  67.6 11.8 %update.1 = f32[64,4096]{1,0:T(8,128)} custom-call(s32[1]{0:T(128)} %bitcast.base_ref, s32[1,512]{1,0:T(1,128)S(1)} %bitcast.9, bf16[4096,1024]{1,0:T(8,128)(2,1)} %emb_ref.3, bf16[512,1024]{1,0:T(8,128)(2,1)S(1)} %get-tuple-element.5.block_ref, f32[8,512]{1,0:T(8,128)S(1)} %get-tuple-element.6.norms_ref, f32[64,512]{1,0:T(8,128)S(1)} %copy-done.3, ...), custom_call_target="tpu_custom_call" | custom-call | tf_op jit(solution)/shard_map/update/pallas_call | solution.py:188
Async XLA Ops:
  0.6 31.9 %copy-start.5 = (s32[512]{0:T(512)S(1)}, s32[512]{0:T(512)}, u32[]{:S(2)}) copy-start(s32[512]{0:T(512)} %ids_ref.1) | copy-start | bytes 6148
  0.6 3.4 %copy-start = (bf16[4096,1024]{1,0:T(8,128)(2,1)S(1)}, bf16[4096,1024]{1,0:T(8,128)(2,1)}, u32[]{:S(2)}) copy-start(bf16[4096,1024]{1,0:T(8,128)(2,1)} %emb_ref.3) | copy-start | bytes 25165828
  4.0 1.2 %copy-start.1 = (f32[4096,64]{0,1:T(8,128)S(1)}, f32[4096,64]{0,1:T(8,128)}, u32[]{:S(2)}) copy-start(f32[4096,64]{0,1:T(8,128)} %param.4) | copy-start | bytes 3145732
  5.3 0.7 copy-start.4
  5.9 60.7 %copy-start.2 = (f32[4096,64]{0,1:T(8,128)S(1)}, f32[4096,64]{0,1:T(8,128)}, u32[]{:S(2)}) copy-start(f32[4096,64]{0,1:T(8,128)} %param.4) | copy-start | bytes 3145732
  66.7 0.9 %copy-start.3 = (f32[64,512]{1,0:T(8,128)S(1)}, f32[64,512]{1,0:T(8,128)}, u32[]{:S(2)}) copy-start(f32[64,512]{1,0:T(8,128)} %get-tuple-element.7.change_ref) | copy-start | bytes 393220

commit v2 on v1

--- a/solution.py
+++ b/solution.py
@@ -9,23 +9,36 @@
 ridge_weight = 0.5
 TILE = 128
 STEP = 8
+PART = 512
+PANEL = 32
 HIGH = lax.Precision.HIGHEST
 
 
+def inverse_of(x):
+    d = pl.reciprocal(x, approx=True)
+    return d * (2.0 - x * d)
+
+
 def small_inverse(entries, n):
-    a = {k: v for k, v in entries.items()}
-    get = lambda i, j: a[(min(i, j), max(i, j))]
-    for k in range(n):
-        d = 1.0 / get(k, k)
-        col = {i: get(i, k) for i in range(n) if i != k}
-        scaled = {i: col[i] * d for i in col}
-        for i in range(n):
-            for j in range(i, n):
-                if i != k and j != k:
-                    a[(i, j)] = a[(i, j)] - scaled[i] * col[j]
-        for i in col:
-            a[(min(i, k), max(i, k))] = scaled[i]
-        a[(k, k)] = -d
+    a = dict(entries)
+    at = lambda i, j: (min(i, j), max(i, j))
+    for k in range(0, n, 2):
+        first, mixed, second = a[k, k], a[k, k + 1], a[k + 1, k + 1]
+        d = inverse_of(first * second - mixed * mixed)
+        p, q, r = second * d, -mixed * d, first * d
+        others = [i for i in range(n) if i not in (k, k + 1)]
+        one = {i: a[at(i, k)] for i in others}
+        two = {i: a[at(i, k + 1)] for i in others}
+        u = {i: p * one[i] + q * two[i] for i in others}
+        v = {i: q * one[i] + r * two[i] for i in others}
+        for i in others:
+            for j in others:
+                if i <= j:
+                    a[i, j] = a[i, j] - (u[i] * one[j] + v[i] * two[j])
+        for i in others:
+            a[at(i, k)] = u[i]
+            a[at(i, k + 1)] = v[i]
+        a[k, k], a[k, k + 1], a[k + 1, k + 1] = -p, -q, -r
     return {k: -v for k, v in a.items()}
 
 
@@ -34,38 +47,51 @@
     sub = lax.broadcasted_iota(jnp.int32, (8, TILE), 0)
     m = list(m)
     groups = TILE // 8
-    for p in range(groups):
-        c0 = p * STEP
-        panel = m[p]
-        entries = {
-            (i, j): jnp.broadcast_to(panel[i:i + 1, c0 + j:c0 + j + 1], (8, TILE))
-            for i in range(STEP) for j in range(i, STEP)
-        }
-        inv = small_inverse(entries, STEP)
-        inside = (lane >= c0) & (lane < c0 + STEP)
-        unit = jnp.where(lane - c0 == sub, 1.0, 0.0)
-        augmented = jnp.where(inside, unit, panel)
-        rows = [jnp.broadcast_to(augmented[j:j + 1, :], (8, TILE)) for j in range(STEP)]
-        new_rows = []
-        for i in range(STEP):
-            acc = None
-            for j in range(STEP):
-                term = inv[(min(i, j), max(i, j))] * rows[j]
-                acc = term if acc is None else acc + term
-            new_rows.append(acc)
-        for v in range(groups):
-            if v == p:
-                continue
-            acc = jnp.where(inside, 0.0, m[v])
-            for j in range(STEP):
-                coef = jnp.broadcast_to(m[v][:, c0 + j:c0 + j + 1], (8, TILE))
-                acc = acc - coef * new_rows[j]
-            m[v] = acc
-        acc = new_rows[0]
-        for j in range(1, STEP):
-            acc = jnp.where(sub == j, new_rows[j], acc)
-        m[p] = acc
+    per = PANEL // 8
+    for q in range(TILE // PANEL):
+        panel_groups = range(q * per, (q + 1) * per)
+        for p in panel_groups:
+            c0 = p * STEP
+            panel = m[p]
+            inside = (lane >= c0) & (lane < c0 + STEP)
+            spread = [jnp.broadcast_to(panel[:, c0 + j:c0 + j + 1], (8, TILE)) for j in range(STEP)]
+            entries = {
+                (i, j): jnp.broadcast_to(spread[j][i:i + 1, :], (8, TILE))
+                for i in range(STEP) for j in range(i, STEP)
+            }
+            inv = small_inverse(entries, STEP)
+            augmented = jnp.where(inside, jnp.where(lane - c0 == sub, 1.0, 0.0), panel)
+            rows = [jnp.broadcast_to(augmented[j:j + 1, :], (8, TILE)) for j in range(STEP)]
+            new_rows = []
+            for i in range(STEP):
+                terms = [inv[(min(i, j), max(i, j))] * rows[j] for j in range(STEP)]
+                new_rows.append(tree_sum(terms))
+            for v in panel_groups:
+                if v == p:
+                    continue
+                terms = [jnp.broadcast_to(m[v][:, c0 + j:c0 + j + 1], (8, TILE)) * new_rows[j] for j in range(STEP)]
+                m[v] = jnp.where(inside, 0.0, m[v]) - tree_sum(terms)
+            acc = new_rows[0]
+            for j in range(1, STEP):
+                acc = jnp.where(sub == j, new_rows[j], acc)
+            m[p] = acc
+        if per < groups:
+            zero = jnp.zeros((8, TILE), jnp.float32)
+            factor_rows = jnp.concatenate([m[v] if v in panel_groups else zero for v in range(groups)], axis=0)
+            others = [v for v in range(groups) if v not in panel_groups]
+            rest = jnp.concatenate([m[v] for v in others], axis=0)
+            lanes = lax.broadcasted_iota(jnp.int32, rest.shape, 1)
+            inside = (lanes >= q * PANEL) & (lanes < (q + 1) * PANEL)
+            rest = jnp.where(inside, 0.0, rest) - dot(jnp.where(inside, rest, 0.0), factor_rows)
+            for at, v in enumerate(others):
+                m[v] = rest[8 * at:8 * at + 8]
     return m
+
+
+def tree_sum(terms):
+    while len(terms) > 1:
+        terms = [terms[t] + terms[t + 1] for t in range(0, len(terms) - 1, 2)] + terms[len(terms) & ~1:]
+    return terms[0]
 
 
 def dot(a, b, dims=((1,), (0,))):
@@ -164,20 +190,29 @@
     )(ids.reshape(1, n), gathered)
 
 
-def update_kernel(base_ref, ids_ref, emb_ref, block_ref, norms_ref, change_ref, res_ref, out_ref):
+def update_kernel(base_ref, ids_ref, emb_ref, block_ref, norms_ref, change_ref, res_ref, out_ref, block_t_ref, change_t_ref):
     step = pl.program_id(0)
     rows, width = emb_ref.shape
-    emb = emb_ref[...]
-    wide = emb.astype(jnp.float32)
-    row_norms = jnp.sum(wide * wide, axis=1, keepdims=True)
-    cross = lax.dot_general(emb, block_ref[...], (((1,), (1,)), ((), ())), preferred_element_type=jnp.float32)
-    dist = jnp.maximum(row_norms + norms_ref[0:1, :] - 2.0 * cross, 0.0)
-    columns = jnp.exp(dist * (-2.0 / width))
-    row = base_ref[0] + step * rows + lax.broadcasted_iota(jnp.int32, (rows, 1), 0)
-    columns = columns + jnp.where(row == ids_ref[...], ridge_weight, 0.0)
-    out_ref[...] = res_ref[...] - lax.dot_general(
-        change_ref[...].astype(jnp.bfloat16), columns.astype(jnp.bfloat16),
-        (((1,), (1,)), ((), ())), preferred_element_type=jnp.float32)
+    rate = 2.0 / width * 1.4426950408889634
+
+    @pl.when(step == 0)
+    def _():
+        block_t_ref[...] = block_ref[...].T
+        change_t_ref[...] = change_ref[...].T.astype(jnp.bfloat16)
+
+    block_norms = norms_ref[0:1, :] * rate
+    ids = ids_ref[...] - (base_ref[0] + step * rows)
+    part = min(rows, PART)
+    for lo in range(0, rows, part):
+        emb = emb_ref[lo:lo + part, :]
+        wide = emb.astype(jnp.float32)
+        row_norms = jnp.sum(wide * wide, axis=1, keepdims=True) * rate
+        cross = jnp.dot(emb, block_t_ref[...], preferred_element_type=jnp.float32)
+        columns = jnp.exp2(jnp.minimum(cross * (2.0 * rate) - (row_norms + block_norms), 0.0))
+        row = lo + lax.broadcasted_iota(jnp.int32, (part, 1), 0)
+        columns = jnp.where(row == ids, columns + ridge_weight, columns)
+        taken = jnp.dot(columns.astype(jnp.bfloat16), change_t_ref[...], preferred_element_type=jnp.float32)
+        out_ref[:, lo:lo + part] = res_ref[:, lo:lo + part] - taken.T
 
 
 def update(base, ids, emb, block, norms, change, res_t, rows_step=512):
@@ -197,7 +232,8 @@
             pl.BlockSpec((outs, rows_step), lambda i: (0, i)),
         ],
         out_specs=pl.BlockSpec((outs, rows_step), lambda i: (0, i)),
-        compiler_params=pltpu.CompilerParams(vmem_limit_bytes=48 * 2**20),
+        scratch_shapes=[pltpu.VMEM((width, n), jnp.bfloat16), pltpu.VMEM((n, outs), jnp.bfloat16)],
+        compiler_params=pltpu.CompilerParams(vmem_limit_bytes=60 * 2**20),
         name="update",
     )(base, ids.reshape(1, n), emb, block, norms, change, res_t)
 
@@ -252,7 +288,7 @@
         ],
         out_specs=pl.BlockSpec(memory_space=pltpu.VMEM),
         scratch_shapes=[pltpu.VMEM((16 * slots, width), jnp.bfloat16), pltpu.SemaphoreType.DMA((slots,))],
-        compiler_params=pltpu.CompilerParams(vmem_limit_bytes=32 * 2**20),
+        compiler_params=pltpu.CompilerParams(vmem_limit_bytes=60 * 2**20),
         name="pack",
     )(base, ids, emb, res_t)
 

time: 79.8 us -> 75.9 us (0.951)
  local copies, waits for them, and re-layouts: 6.19 us -> 2.44 us
    unnamed x12 -> x8, local copies, waits for them, and re-layouts: 6.19 us -> 2.44 us
    pallas_call x1, Pallas kernels: 3.41 us -> 5.53 us  [pack(): pl.pallas_call(pack_kernel, out_shape=jax.ShapeDtypeStruct((slots, width...]
    pallas_call x1, Pallas kernels: 34.2 us -> 32.1 us  [solve(): pl.pallas_call(functools.partial(solve_kernel, rows_here, capacity), out_...]
where the time goes in v2:
time: 75.9 us; the launch traced here: 75.6 us
  Pallas kernels  72.5 us (96%)
  local copies, waits for them, and re-layouts  2.44 us (3%)
    pallas_call x1, Pallas kernels, solve(): pl.pallas_call(functools.partial(solve_kernel, rows_here, capacity), out_...  32.1 us
    pallas_call x1, Pallas kernels, gather(): pl.pallas_call(functools.partial(gather_kernel, (n_far, n_side)), out_sha...  22.8 us
    pallas_call x1, Pallas kernels, update(): pl.pallas_call(update_kernel, grid=(rows // rows_step,), out_shape=jax.Sh...  12.1 us
    pallas_call x1, Pallas kernels, pack(): pl.pallas_call(pack_kernel, out_shape=jax.ShapeDtypeStruct((slots, width...  5.53 us
    unnamed x8, local copies, waits for them, and re-layouts  2.44 us

profile of v2, /device:TPU:0, one launch (start us, length us, event | category | flops | bytes accessed | tf_op | source)
XLA Modules:
  0.0 75.6 jit_solution(10454533330711873086)
XLA Ops:
  0.6 0.0 copy-start.2
  0.6 5.5 %pack.1.packed_ref = bf16[32,1152]{1,0:T(8,128)(2,1)} custom-call(s32[1]{0:T(128)} %bitcast.base_ref, s32[512]{0:T(512)} %ids_ref.1, bf16[4096,1024]{1,0:T(8,128)(2,1)} %emb_ref.3, f32[64,4096]{1,0:T(8,128)} %bitcast.7), custom_call_target="tpu_custom_call" | custom-call | tf_op jit(solution)/shard_map/pack/pallas_call | solution.py:282
  6.2 0.0 copy-start.1
  6.2 0.9 %copy-done.1 = bf16[32,1152]{1,0:T(8,128)(2,1)S(1)} copy-done((bf16[32,1152]{1,0:T(8,128)(2,1)S(1)}, bf16[32,1152]{1,0:T(8,128)(2,1)}, u32[]{:S(2)}) %copy-start.1) | copy-done | bytes 73752
  7.1 22.8 %gather.1.gathered_ref = bf16[1024,1152]{1,0:T(8,128)(2,1)S(1)} custom-call(bf16[32,1152]{1,0:T(8,128)(2,1)S(1)} %copy-done.1), custom_call_target="tpu_custom_call" | custom-call | tf_op jit(solution)/shard_map/gather/pallas_call | solution.py:383
  29.9 0.0 copy-done.2
  29.9 32.1 %solve.1 = (bf16[512,1024]{1,0:T(8,128)(2,1)S(1)}, f32[8,512]{1,0:T(8,128)S(1)}, f32[64,512]{1,0:T(8,128)}) custom-call(s32[1,512]{1,0:T(1,128)S(1)} %bitcast.6, bf16[1024,1152]{1,0:T(8,128)(2,1)S(1)} %gather.1.gathered_ref), custom_call_target="tpu_custom_call" | custom-call | tf_op jit(solution)/shard_map/solve/pallas_call | solution.py:174
  61.9 0.0 copy-start
  61.9 1.0 %copy-done = bf16[512,1024]{1,0:T(8,128)(2,1)} copy-done((bf16[512,1024]{1,0:T(8,128)(2,1)}, bf16[512,1024]{1,0:T(8,128)(2,1)S(1)}, u32[]{:S(2)}) %copy-start) | copy-done | bytes 1048600
  62.9 0.0 copy-start.3
  62.9 0.6 copy-done.3
  63.5 12.1 %update.1 = f32[64,4096]{1,0:T(8,128)} custom-call(s32[1]{0:T(128)} %bitcast.base_ref, s32[1,512]{1,0:T(1,128)} %bitcast.5, bf16[4096,1024]{1,0:T(8,128)(2,1)} %emb_ref.3, bf16[512,1024]{1,0:T(8,128)(2,1)} %copy-done, f32[8,512]{1,0:T(8,128)} %copy-done.3, f32[64,512]{1,0:T(8,128)} %get-tuple-element.7.change_ref, f32[64,4096]{1,0:T(8,128)} %bitcast.8), custom_call_target="tpu_custom_call" | custom-call | tf_op jit(solution)/shard_map/update/pallas_call | solution.py:223
Async XLA Ops:
  0.6 29.2 %copy-start.2 = (s32[512]{0:T(512)S(1)}, s32[512]{0:T(512)}, u32[]{:S(2)}) copy-start(s32[512]{0:T(512)} %ids_ref.1) | copy-start | bytes 6148
  6.2 0.9 %copy-start.1 = (bf16[32,1152]{1,0:T(8,128)(2,1)S(1)}, bf16[32,1152]{1,0:T(8,128)(2,1)}, u32[]{:S(2)}) copy-start(bf16[32,1152]{1,0:T(8,128)(2,1)} %pack.1.packed_ref) | copy-start | bytes 221188
  61.9 1.0 %copy-start = (bf16[512,1024]{1,0:T(8,128)(2,1)}, bf16[512,1024]{1,0:T(8,128)(2,1)S(1)}, u32[]{:S(2)}) copy-start(bf16[512,1024]{1,0:T(8,128)(2,1)S(1)} %get-tuple-element.5.block_ref) | copy-start | bytes 3145732
  62.9 0.6 copy-start.3

commit v3 on v2

--- a/solution.py
+++ b/solution.py
@@ -142,23 +142,19 @@
     tiles = n // TILE
     groups = TILE // 8
 
-    def factor(k, carry):
-        here = pl.ds(pl.multiple_of(k * TILE, TILE), TILE)
-        m = [a_ref[pl.ds(pl.multiple_of(k * TILE + 8 * v, 8), 8), here] for v in range(groups)]
-        m = tile_inverse(m)
+    for k in range(tiles):
+        lo, hi = k * TILE, (k + 1) * TILE
+        m = tile_inverse([a_ref[lo + 8 * v:lo + 8 * v + 8, lo:hi] for v in range(groups)])
         for v in range(groups):
             inv_ref[k, 8 * v:8 * v + 8, :] = m[v]
-        inv = inv_ref[k]
-        right = a_ref[here, :]
-        scaled = dot(inv, right)
-        scaled_res = dot(inv, r_ref[here, :])
-        rows_after = lax.broadcasted_iota(jnp.int32, (n, 1), 0) >= (k + 1) * TILE
-        left = jnp.where(rows_after, a_ref[:, here], 0.0)
-        a_ref[...] = a_ref[...] - dot(left, scaled)
-        r_ref[...] = r_ref[...] - dot(left, scaled_res)
-        return carry
-
-    lax.fori_loop(0, tiles, factor, 0)
+        if hi < n:
+            inv = inv_ref[k]
+            left = a_ref[hi:, lo:hi]
+            scaled = dot(inv, a_ref[lo:hi, hi:])
+            scaled_res = dot(inv, r_ref[lo:hi, :])
+            a_ref[hi:, hi:] = a_ref[hi:, hi:] - dot(left, scaled)
+            r_ref[hi:, :] = r_ref[hi:, :] - dot(left, scaled_res)
+
     for k in range(tiles - 1, -1, -1):
         lo, hi = k * TILE, (k + 1) * TILE
         rest = r_ref[lo:hi, :]

time: 75.9 us -> 71.3 us (0.939)
  Pallas kernels: 72.5 us -> 68 us
    pallas_call x1, Pallas kernels: 32.1 us -> 27.9 us  [solve(): pl.pallas_call(functools.partial(solve_kernel, rows_here, capacity), out_...]
where the time goes in v3:
time: 71.3 us; the launch traced here: 71.1 us
  Pallas kernels  68 us (95%)
  local copies, waits for them, and re-layouts  2.44 us (3%)
    pallas_call x1, Pallas kernels, solve(): pl.pallas_call(functools.partial(solve_kernel, rows_here, capacity), out_...  27.9 us
    pallas_call x1, Pallas kernels, gather(): pl.pallas_call(functools.partial(gather_kernel, (n_far, n_side)), out_sha...  22.8 us
    pallas_call x1, Pallas kernels, update(): pl.pallas_call(update_kernel, grid=(rows // rows_step,), out_shape=jax.Sh...  12.1 us
    pallas_call x1, Pallas kernels, pack(): pl.pallas_call(pack_kernel, out_shape=jax.ShapeDtypeStruct((slots, width...  5.15 us
    unnamed x8, local copies, waits for them, and re-layouts  2.44 us

profile of v3, /device:TPU:0, one launch (start us, length us, event | category | flops | bytes accessed | tf_op | source)
XLA Modules:
  0.0 71.1 jit_solution(8854782684950833568)
XLA Ops:
  0.6 0.0 copy-start.2
  0.6 5.2 %pack.1.packed_ref = bf16[32,1152]{1,0:T(8,128)(2,1)} custom-call(s32[1]{0:T(128)} %bitcast.base_ref, s32[512]{0:T(512)} %ids_ref.1, bf16[4096,1024]{1,0:T(8,128)(2,1)} %emb_ref.3, f32[64,4096]{1,0:T(8,128)} %bitcast.7), custom_call_target="tpu_custom_call" | custom-call | tf_op jit(solution)/shard_map/pack/pallas_call | solution.py:278
  5.8 0.0 copy-start.1
  5.8 0.9 %copy-done.1 = bf16[32,1152]{1,0:T(8,128)(2,1)S(1)} copy-done((bf16[32,1152]{1,0:T(8,128)(2,1)S(1)}, bf16[32,1152]{1,0:T(8,128)(2,1)}, u32[]{:S(2)}) %copy-start.1) | copy-done | bytes 73752
  6.7 22.8 %gather.1.gathered_ref = bf16[1024,1152]{1,0:T(8,128)(2,1)S(1)} custom-call(bf16[32,1152]{1,0:T(8,128)(2,1)S(1)} %copy-done.1), custom_call_target="tpu_custom_call" | custom-call | tf_op jit(solution)/shard_map/gather/pallas_call | solution.py:379
  29.5 0.0 copy-done.2
  29.5 27.9 %solve.1 = (bf16[512,1024]{1,0:T(8,128)(2,1)S(1)}, f32[8,512]{1,0:T(8,128)S(1)}, f32[64,512]{1,0:T(8,128)}) custom-call(s32[1,512]{1,0:T(1,128)S(1)} %bitcast.6, bf16[1024,1152]{1,0:T(8,128)(2,1)S(1)} %gather.1.gathered_ref), custom_call_target="tpu_custom_call" | custom-call | tf_op jit(solution)/shard_map/solve/pallas_call | solution.py:170
  57.4 0.0 copy-start
  57.4 1.0 %copy-done = bf16[512,1024]{1,0:T(8,128)(2,1)} copy-done((bf16[512,1024]{1,0:T(8,128)(2,1)}, bf16[512,1024]{1,0:T(8,128)(2,1)S(1)}, u32[]{:S(2)}) %copy-start) | copy-done | bytes 1048600
  58.4 0.0 copy-start.3
  58.4 0.6 copy-done.3
  59.0 12.1 %update.1 = f32[64,4096]{1,0:T(8,128)} custom-call(s32[1]{0:T(128)} %bitcast.base_ref, s32[1,512]{1,0:T(1,128)} %bitcast.5, bf16[4096,1024]{1,0:T(8,128)(2,1)} %emb_ref.3, bf16[512,1024]{1,0:T(8,128)(2,1)} %copy-done, f32[8,512]{1,0:T(8,128)} %copy-done.3, f32[64,512]{1,0:T(8,128)} %get-tuple-element.7.change_ref, f32[64,4096]{1,0:T(8,128)} %bitcast.8), custom_call_target="tpu_custom_call" | custom-call | tf_op jit(solution)/shard_map/update/pallas_call | solution.py:219
Async XLA Ops:
  0.6 28.9 %copy-start.2 = (s32[512]{0:T(512)S(1)}, s32[512]{0:T(512)}, u32[]{:S(2)}) copy-start(s32[512]{0:T(512)} %ids_ref.1) | copy-start | bytes 6148
  5.8 0.9 %copy-start.1 = (bf16[32,1152]{1,0:T(8,128)(2,1)S(1)}, bf16[32,1152]{1,0:T(8,128)(2,1)}, u32[]{:S(2)}) copy-start(bf16[32,1152]{1,0:T(8,128)(2,1)} %pack.1.packed_ref) | copy-start | bytes 221188
  57.4 1.0 %copy-start = (bf16[512,1024]{1,0:T(8,128)(2,1)}, bf16[512,1024]{1,0:T(8,128)(2,1)S(1)}, u32[]{:S(2)}) copy-start(bf16[512,1024]{1,0:T(8,128)(2,1)S(1)} %get-tuple-element.5.block_ref) | copy-start | bytes 3145732
  58.4 0.6 copy-start.3
